TPU v7x, 128 devices: a whole 4x4x4 slice. The times are simulated.
128 devices in a mesh: group: 4 (over y), dev: 32 (over x, z, core).
Axes of the slice: x: 4, y: 4, z: 4, core: 2. Of those that a mesh axis runs over, the one named last changes fastest.
Arguments:
- a_tiles: bfloat16 [4096, 2, 2, 256, 256], P(('group', 'dev')), may hold values from -4 to 4
- scaling: float32 [4096, 2, 256], P(('group', 'dev')), may hold values from 0.2 to 5
- dest_owner: int32 [4096, 1], P(('group', 'dev')), may hold values from 0 to 31; in each aligned block of 32 rows (0 to 31, 32 to 63, ...) at most 2 rows name the same one
- dest_slot: int32 [4096], P(('group', 'dev')), may hold values from 0 to 15
- panel: bfloat16 [8192, 512], P('dev', 'group'), may hold values from -3.59375 to 3.59375
- front_tiles: int32 [512, 2], P(('group', 'dev')), may hold values from 0 to 31
Outputs:
- schur: float32 [512, 256, 256], P(('group', 'dev'))
Inputs may be any that keep to these rules, and one draw needn't show every extreme that they name: `dest_owner`: among the 32 contributions of one device, no owner is named more than 2 times, a bound that some block reaches.
All inputs are finite; a program needn't handle non-finite values.
Results may differ from a plain program's by a relative error of at most 0.0031.
Values may be sent and summed in bfloat16 or wider, within the bound.
No kernel may reach another device: no remote copies, remote signals or barrier semaphores. Data moves between devices by JAX's collectives and lax.ppermute only.
A program may use at most 128 MiB of HBM per device.

v0:
```python
import functools
import jax
import jax.numpy as jnp
from jax import lax
from jax.experimental import pallas as pl
from jax.experimental.pallas import tpu as pltpu
from jax.sharding import PartitionSpec as P

AXES = ("group", "chip", "core")
PLANE = ("group", "chip")
LANES = 128
BATCH = 16
VMEM = pltpu.CompilerParams(vmem_limit_bytes=48 << 20)


def exchange(x, axes):
    return lax.all_to_all(x, axes, split_axis=0, concat_axis=0, tiled=True)


def device_of(i, j, n_across):
    return (i // 2) * (2 * n_across) + 2 * j + i % 2


def swap_matrix(per):
    cols = LANES // per
    width = per * LANES
    source = lax.broadcasted_iota(jnp.int32, (width, width), 0)
    dest = lax.broadcasted_iota(jnp.int32, (width, width), 1)
    swapped = (dest // cols % per) * LANES + dest // LANES * cols + dest % cols
    return (source == swapped).astype(jnp.bfloat16)


def early_kernel(n_down, n_across, owner_hbm, slot_hbm, front_hbm, panel_hbm, out_ref,
                 owner_ref, slot_ref, front_ref, panel_ref, sem_ref):
    pairs = [(owner_hbm, owner_ref), (slot_hbm, slot_ref), (front_hbm, front_ref), (panel_hbm, panel_ref)]
    copies = [pltpu.make_async_copy(a, b, sem_ref.at[n]) for n, (a, b) in enumerate(pairs)]
    for copy in copies:
        copy.start()
    for copy in copies:
        copy.wait()
    tile, depth = panel_ref.shape
    rows = tile // n_down
    count = owner_ref.shape[0]
    held = front_ref.shape[1]
    lane = lax.broadcasted_iota(jnp.int32, (8, depth), 1)
    numbers = jnp.zeros((8, depth), jnp.int32)
    for c in range(count):
        numbers = jnp.where(lane == c, owner_ref[c], numbers)
        numbers = jnp.where(lane == count + c, slot_ref[c], numbers)
    for s in range(held):
        for side in range(2):
            numbers = jnp.where(lane == 2 * count + side * held + s, front_ref[side, s], numbers)
    numbers = numbers.astype(jnp.float32).astype(jnp.bfloat16)
    cols = tile // n_across
    for a in range(n_down // 2):
        for j in range(n_across):
            chip = a * n_across + j
            out_ref[chip, 0:2 * rows, :] = panel_ref[2 * a * rows:2 * (a + 1) * rows, :]
            out_ref[chip, 2 * rows:2 * rows + cols, :] = panel_ref[j * cols:(j + 1) * cols, :]
            out_ref[chip, 2 * rows + cols:2 * rows + cols + 8, :] = numbers


def early_blocks(owner, slot, front_tiles, panel, n_down, n_across):
    tile, depth = panel.shape
    height = 2 * (tile // n_down) + tile // n_across + 8
    front = front_tiles.T
    hbm = pl.BlockSpec(memory_space=pltpu.HBM)
    return pl.pallas_call(
        functools.partial(early_kernel, n_down, n_across),
        in_specs=[hbm] * 4,
        out_specs=pl.BlockSpec(memory_space=pltpu.VMEM),
        out_shape=jax.ShapeDtypeStruct((n_down * n_across // 2, height, depth), jnp.bfloat16),
        scratch_shapes=[
            pltpu.SMEM(owner.shape, owner.dtype),
            pltpu.SMEM(slot.shape, slot.dtype),
            pltpu.SMEM(front.shape, front.dtype),
            pltpu.VMEM(panel.shape, panel.dtype),
            pltpu.SemaphoreType.DMA((4,)),
        ],
        compiler_params=pltpu.CompilerParams(vmem_limit_bytes=64 << 20),
    )(owner, slot, front, panel)


def products_kernel(n_down, n_across, a_ref, scale_ref, swap_ref, out_ref, held_ref):
    count, blocks, _, tile, _ = a_ref.shape
    rows, cols = tile // n_down, tile // n_across
    per = LANES // cols
    quads = rows // per
    sides = tile // LANES
    step = pl.program_id(1)
    for u in range(count):
        total = None
        for k in range(blocks):
            scaled = (a_ref[u, k, 0].astype(jnp.float32) * scale_ref[u, k][None, :]).astype(jnp.bfloat16)
            part = lax.dot_general(
                scaled, a_ref[u, k, 1], (((1,), (1,)), ((), ())), preferred_element_type=jnp.float32
            )
            total = part if total is None else total + part
        for h in range(sides):
            held_ref[h, pl.ds(step * count + u, tile, stride=BATCH), :] = total[:, h * LANES:(h + 1) * LANES]

    @pl.when(step == pl.num_programs(1) - 1)
    def _():
        together = 4

        @pl.loop(0, n_down // together)
        def _(block):
            at = [(d, q, h) for d in range(together) for q in range(quads) for h in range(sides)]
            parts = []
            for d, q, h in at:
                row = ((block * together + d) * rows + q * per) * BATCH
                parts.append(jnp.concatenate([
                    held_ref[h, pl.ds(pl.multiple_of(row + r * BATCH, BATCH), BATCH), :].astype(jnp.bfloat16)
                    for r in range(per)
                ], axis=1))
            swapped = jnp.dot(
                jnp.concatenate(parts, axis=0), swap_ref[...], preferred_element_type=jnp.float32
            ).astype(jnp.bfloat16)
            for n, (d, q, h) in enumerate(at):
                for j in range(per):
                    first = block * (together * n_across) + device_of(d, h * per + j, n_across)
                    out_ref[first, :, q * LANES:(q + 1) * LANES] = (
                        swapped[n * BATCH:(n + 1) * BATCH, j * LANES:(j + 1) * LANES]
                    )


def form_products(a_tiles, scaling, swap, n_down, n_across):
    contribs, blocks, _, tile, _ = a_tiles.shape
    n_all = n_down * n_across
    chunk = tile * tile // n_all
    count = 8
    steps = BATCH // count
    return pl.pallas_call(
        functools.partial(products_kernel, n_down, n_across),
        grid=(contribs // BATCH, steps),
        in_specs=[
            pl.BlockSpec((count, blocks, 2, tile, tile), lambda g, s: (g * steps + s, 0, 0, 0, 0)),
            pl.BlockSpec((count, blocks, tile), lambda g, s: (g * steps + s, 0, 0)),
            pl.BlockSpec(swap.shape, lambda g, s: (0, 0)),
        ],
        out_specs=pl.BlockSpec((n_all, BATCH, chunk), lambda g, s: (0, g, 0)),
        out_shape=jax.ShapeDtypeStruct((n_all, contribs, chunk), jnp.bfloat16),
        scratch_shapes=[pltpu.VMEM((tile // LANES, tile * BATCH, LANES), jnp.float32)],
        compiler_params=VMEM,
    )(a_tiles, scaling, swap)


def sum_kernel(x_ref, target_ref, update_ref, out_ref, total_ref, spread_ref):
    step = pl.program_id(0)
    n_tiles, chunk = total_ref.shape
    number = lax.broadcasted_iota(jnp.int32, (n_tiles, x_ref.shape[0]), 0)
    picking = (number == target_ref[...]).astype(jnp.float32).astype(jnp.bfloat16)
    part = jnp.dot(picking, x_ref[...], preferred_element_type=jnp.float32)

    @pl.when(step == 0)
    def _():
        total_ref[...] = part - update_ref[...]

    @pl.when(step > 0)
    def _():
        total_ref[...] += part

    @pl.when(step == pl.num_programs(0) - 1)
    def _():
        pieces = chunk // LANES
        for q in range(pieces):
            spread_ref[pl.ds(q, n_tiles, stride=pieces), :] = total_ref[:, q * LANES:(q + 1) * LANES]
        out_ref[...] = spread_ref[...].astype(jnp.bfloat16)


def sum_by_target(x, target, update):
    contribs, chunk = x.shape
    n_tiles = update.shape[0]
    block = 1024
    return pl.pallas_call(
        sum_kernel,
        grid=(contribs // block,),
        in_specs=[
            pl.BlockSpec((block, chunk), lambda s: (s, 0)),
            pl.BlockSpec((1, block), lambda s: (0, s)),
            pl.BlockSpec((n_tiles, chunk), lambda s: (0, 0)),
        ],
        out_specs=pl.BlockSpec((n_tiles * chunk // LANES, LANES), lambda s: (0, 0)),
        out_shape=jax.ShapeDtypeStruct((n_tiles * chunk // LANES, LANES), jnp.bfloat16),
        scratch_shapes=[
            pltpu.VMEM((n_tiles, chunk), jnp.float32),
            pltpu.VMEM((n_tiles * chunk // LANES, LANES), jnp.float32),
        ],
        compiler_params=VMEM,
    )(x, target.reshape(1, -1), update)


def final_kernel(n_down, n_across, x_ref, swap_ref, out_ref, spread_ref):
    held, tile, _ = out_ref.shape
    rows, cols = tile // n_down, tile // n_across
    per = LANES // cols
    quads = rows // per
    sides = tile // LANES
    at = [(i, h) for i in range(n_down) for h in range(sides)]
    parts = []
    for i, h in at:
        parts.append(jnp.concatenate([x_ref[device_of(i, h * per + j, n_across)] for j in range(per)], axis=1))
    swapped = jnp.dot(jnp.concatenate(parts, axis=0), swap_ref[...], preferred_element_type=jnp.float32)
    for n, (i, h) in enumerate(at):
        for r in range(per):
            for s in range(held):
                top = n * held * quads + s * quads
                spread_ref[h, pl.ds(s * tile + i * rows + r, quads, stride=per), :] = (
                    swapped[top:top + quads, r * LANES:(r + 1) * LANES]
                )
    for s in range(held):
        for h in range(sides):
            out_ref[s, :, h * LANES:(h + 1) * LANES] = spread_ref[h, s * tile:(s + 1) * tile, :]


def final_tiles(x, swap, tile, held, n_down, n_across):
    vmem = pl.BlockSpec(memory_space=pltpu.VMEM)
    return pl.pallas_call(
        functools.partial(final_kernel, n_down, n_across),
        in_specs=[vmem, vmem],
        out_specs=vmem,
        out_shape=jax.ShapeDtypeStruct((held, tile, tile), jnp.float32),
        scratch_shapes=[pltpu.VMEM((tile // LANES, held * tile, LANES), jnp.float32)],
        compiler_params=VMEM,
    )(x, swap)


def per_device(a_tiles, scaling, dest_owner, dest_slot, panel, front_tiles):
    contribs, _, _, tile, _ = a_tiles.shape
    n_group, n_chip, n_core = (lax.axis_size(name) for name in AXES)
    n_dev = n_chip * n_core
    n_all = n_dev * n_group
    held = front_tiles.shape[0]
    n_tiles = n_all * held
    n_across = 8
    n_down = n_all // n_across
    rows, cols = tile // n_down, tile // n_across
    chunk = rows * cols
    depth = panel.shape[1]
    swap = swap_matrix(LANES // cols)

    early = exchange(early_blocks(dest_owner[:, 0], dest_slot, front_tiles, panel, n_down, n_across), PLANE)
    arrived = exchange(form_products(a_tiles, scaling, swap, n_down, n_across), AXES)

    even = lax.axis_index("core") == 0
    low, high, rest = early[:, :rows], early[:, rows:2 * rows], early[:, 2 * rows:]
    own = jnp.concatenate([jnp.where(even, low, high), rest], axis=1)
    other = jnp.concatenate([jnp.where(even, high, low), rest], axis=1)
    other = lax.ppermute(other, "core", [(0, 1), (1, 0)])
    early = jnp.where(even, jnp.stack([own, other], axis=1), jnp.stack([other, own], axis=1))
    early = early.reshape(n_group, n_dev, -1, depth)

    numbers = early[:, :, rows + cols].astype(jnp.int32).reshape(n_all, depth)
    owner, slot = numbers[:, :contribs].reshape(-1), numbers[:, contribs:2 * contribs].reshape(-1)
    target = (slot // held) * (n_dev * held) + owner * held + slot % held
    first = 2 * contribs
    row_piece = numbers[:, first:first + held].reshape(-1)
    col_piece = numbers[:, first + held:first + 2 * held].reshape(-1)

    grid = jnp.einsum(
        "glrp,gsmp->lsrm", early[:, :, :rows], early[:, :, rows:rows + cols], preferred_element_type=jnp.float32
    ).reshape(n_dev * n_dev, chunk)
    update = jnp.take(grid, row_piece * n_dev + col_piece, axis=0, mode="clip")

    sums = sum_by_target(arrived.reshape(n_all * contribs, chunk), target, update)
    final = exchange(sums.reshape(n_all, held * chunk // LANES, LANES), AXES)
    return final_tiles(final, swap, tile, held, n_down, n_across)


def solution(mesh):
    n_group, n_dev = mesh.devices.shape
    mesh = jax.sharding.Mesh(mesh.devices.reshape(n_group, n_dev // 2, 2), AXES)
    in_specs = (
        P(AXES, None, None, None, None),
        P(AXES, None, None),
        P(AXES, None),
        P(AXES),
        P(("chip", "core"), "group"),
        P(AXES, None),
    )
    out_specs = P(AXES, None, None)
    return jax.shard_map(
        per_device, mesh=mesh, in_specs=in_specs, out_specs=out_specs, check_vma=False
    )
```

profile of v0, /device:TPU:1, one launch (start us, length us, event | category | flops | bytes accessed | tf_op | source)
XLA Modules:
  0.0 117.1 jit_solution(2799665645399412865)
XLA Ops:
  0.0 2.1 %shard_map.65 = bf16[64,72,128]{2,1,0:T(8,128)(2,1)} custom-call(s32[32]{0:T(128)} %bitcast.32, s32[32]{0:T(128)} %slot_hbm.1, s32[2,4]{1,0:T(2,128)} %bitcast.31, bf16[256,128]{1,0:T(8,128)(2,1)} %panel_hbm.1), custom_call_target="tpu_custom_call" | custom-call | tf_op jit(solution)/shard_map/pallas_call | solution.py:68
  2.1 0.0 copy-start.1
  2.1 12.1 %all-to-all-start.1 = ((bf16[64,72,128]{2,1,0:T(8,128)(2,1)}), bf16[64,72,128]{2,1,0:T(8,128)(2,1)S(1)}, u32[]{:S(2)}, u32[]{:S(2)}) async-start(bf16[64,72,128]{2,1,0:T(8,128)(2,1)} %shard_map.65), calls=%async_computation.1 | async-start | bytes 2359296 | tf_op jit(solution)/shard_map/all_to_all | solution.py:17
  14.3 0.1 fusion.5.swap_ref
  14.4 0.0 copy-done.1
  14.4 11.9 %shard_map.64 = bf16[128,32,512]{2,1,0:T(8,128)(2,1)S(1)} custom-call(bf16[32,2,2,256,256]{4,3,2,1,0:T(8,128)(2,1)} %a_ref.1, f32[32,2,256]{2,1,0:T(2,128)S(1)} %copy-done.1, bf16[512,512]{1,0:T(8,128)(2,1)S(1)} %fusion.5.swap_ref), custom_call_target="tpu_custom_call" | custom-call | tf_op jit(solution)/shard_map/pallas_call | solution.py:133
  26.3 0.0 copy-start
  26.3 1.9 %copy-done = bf16[128,32,512]{2,1,0:T(8,128)(2,1)} copy-done((bf16[128,32,512]{2,1,0:T(8,128)(2,1)}, bf16[128,32,512]{2,1,0:T(8,128)(2,1)S(1)}, u32[]{:S(2)}) %copy-start) | copy-done | bytes 4194328
  28.3 4.5 %all-to-all-done.1 = bf16[64,72,128]{2,1,0:T(8,128)(2,1)S(1)} async-done(((bf16[64,72,128]{2,1,0:T(8,128)(2,1)}), bf16[64,72,128]{2,1,0:T(8,128)(2,1)S(1)}, u32[]{:S(2)}, u32[]{:S(2)}) %all-to-all-start.1) | async-done | bytes 1179680 | tf_op jit(solution)/shard_map/all_to_all | solution.py:17
  32.7 7.0 %all-to-all-start = ((bf16[128,32,512]{2,1,0:T(8,128)(2,1)}), bf16[128,32,512]{2,1,0:T(8,128)(2,1)}, u32[]{:S(2)}, u32[]{:S(2)}) async-start(bf16[128,32,512]{2,1,0:T(8,128)(2,1)} %copy-done), calls=%async_computation | async-start | bytes 8388608 | tf_op jit(solution)/shard_map/all_to_all | solution.py:17
  39.8 0.1 slice.44
  39.9 0.2 fusion.6
  40.1 1.4 %collective-permute-start = (bf16[64,56,128]{2,1,0:T(8,128)(2,1)S(1)}, bf16[64,56,128]{2,1,0:T(8,128)(2,1)S(1)}, u32[]{:S(2)}, u32[]{:S(2)}) collective-permute-start(bf16[64,56,128]{2,1,0:T(8,128)(2,1)S(1)} %get-tuple-element.8), channel_id=1, source_target_pairs={{0,1},{1,0},{2,3},{3,2},{4,5},{5,4},{6,7},{7,6},{8,9},{9,8},{10,11... | collective-permute-start | bytes 2752520 | tf_op jit(solution)/shard_map/ppermute | solution.py:249
  41.5 2.1 %collective-permute-done = bf16[64,56,128]{2,1,0:T(8,128)(2,1)S(1)} collective-permute-done((bf16[64,56,128]{2,1,0:T(8,128)(2,1)S(1)}, bf16[64,56,128]{2,1,0:T(8,128)(2,1)S(1)}, u32[]{:S(2)}, u32[]{:S(2)}) %collective-permute-start) | collective-permute-done | bytes 917536 | tf_op jit(solution)/shard_map/ppermute | solution.py:249
  43.6 0.3 maximum_select_fusion
  43.9 0.1 copy.8
  44.1 4.6 %convolution_bitcast_fusion = f32[32,32,16,32]{0,3,2,1:T(8,128)} fusion(bf16[4,32,16,128]{3,2,1,0:T(8,128)(2,1)S(1)} %slice.49, bf16[4,32,56,128]{3,2,1,0:T(8,128)(2,1)S(1)} %bitcast.26), kind=kOutput, calls=%fused_computation.1 | convolution fusion | flops 536870912 | bytes 3670016 | tf_op jit(solution)/shard_map/glrp,gsmp->lsrm/dot_general | solution.py:260
  48.7 9.0 %copy.11 = f32[32,32,16,32]{3,2,1,0:T(8,128)} copy(f32[32,32,16,32]{0,3,2,1:T(8,128)} %convolution_bitcast_fusion) | data formatting | bytes 4194304 | tf_op jit(solution)/shard_map/glrp,gsmp->lsrm/transpose | solution.py:260
  57.7 7.3 %reshape.166 = f32[1024,512]{1,0:T(8,128)} reshape(f32[32,32,16,32]{3,2,1,0:T(8,128)} %copy.11) | data formatting | bytes 4194304 | tf_op jit(solution)/shard_map/reshape | solution.py:262
  65.0 0.1 slice_convert_fusion
  65.1 0.1 slice_add_fusion
  65.2 0.1 reshape.171
  65.3 0.1 fusion.16
  65.4 0.1 mul.61
  65.5 0.1 reshape.165
  65.6 3.6 %gather_fusion = f32[512,512]{1,0:T(8,128)S(1)} fusion(f32[1024,512]{1,0:T(8,128)} %reshape.166, s32[1024]{0:T(1024)S(1)} %pad_clamp_fusion), kind=kCustom, calls=%fused_computation | custom fusion | bytes 2099200 | tf_op jit(solution)/shard_map/jit(_take)/gather | solution.py:263
  69.2 0.1 fusion.7.target_ref
  69.4 23.2 %all-to-all-done = bf16[128,32,512]{2,1,0:T(8,128)(2,1)} async-done(((bf16[128,32,512]{2,1,0:T(8,128)(2,1)}), bf16[128,32,512]{2,1,0:T(8,128)(2,1)}, u32[]{:S(2)}, u32[]{:S(2)}) %all-to-all-start) | async-done | bytes 4194336 | tf_op jit(solution)/shard_map/all_to_all | solution.py:17
  92.5 5.1 %shard_map.66 = bf16[2048,128]{1,0:T(8,128)(2,1)S(1)} custom-call(bf16[4096,512]{1,0:T(8,128)(2,1)} %bitcast.x_ref, s32[1,4096]{1,0:T(1,128)S(1)} %fusion.7.target_ref, f32[512,512]{1,0:T(8,128)S(1)} %gather_fusion), custom_call_target="tpu_custom_call" | custom-call | tf_op jit(solution)/shard_map/pallas_call | solution.py:175
  97.6 17.9 %all_to_all.15.x_ref = bf16[128,16,128]{2,1,0:T(8,128)(2,1)S(1)} all-to-all(bf16[128,16,128]{2,1,0:T(8,128)(2,1)S(1)} %bitcast.24), channel_id=1, replica_groups=mesh['group'=4,'chip'=16,'core'=2] {'group','chip','core'}, dimensions={0} | all-to-all | bytes 1048576 | tf_op jit(solution)/shard_map/all_to_all | solution.py:17
  115.5 1.6 %shard_map.67 = f32[4,256,256]{2,1,0:T(8,128)} custom-call(bf16[128,16,128]{2,1,0:T(8,128)(2,1)S(1)} %all_to_all.15.x_ref, bf16[512,512]{1,0:T(8,128)(2,1)S(1)} %fusion.5.swap_ref), custom_call_target="tpu_custom_call" | custom-call | tf_op jit(solution)/shard_map/pallas_call | solution.py:218
  (8 shorter events, 0.1 us)
Async XLA Ops:
  2.1 12.3 %copy-start.1 = (f32[32,2,256]{2,1,0:T(2,128)S(1)}, f32[32,2,256]{2,1,0:T(2,128)}, u32[]{:S(2)}) copy-start(f32[32,2,256]{2,1,0:T(2,128)} %scale_ref.1) | copy-start | bytes 196612
  2.1 30.7 %all-to-all-start.1 = ((bf16[64,72,128]{2,1,0:T(8,128)(2,1)}), bf16[64,72,128]{2,1,0:T(8,128)(2,1)S(1)}, u32[]{:S(2)}, u32[]{:S(2)}) async-start(bf16[64,72,128]{2,1,0:T(8,128)(2,1)} %shard_map.65), calls=%async_computation.1 | async-start | bytes 2359296 | tf_op jit(solution)/shard_map/all_to_all | solution.py:17
  26.3 1.9 %copy-start = (bf16[128,32,512]{2,1,0:T(8,128)(2,1)}, bf16[128,32,512]{2,1,0:T(8,128)(2,1)S(1)}, u32[]{:S(2)}) copy-start(bf16[128,32,512]{2,1,0:T(8,128)(2,1)S(1)} %shard_map.64) | copy-start | bytes 12582916
  32.7 59.8 %all-to-all-start = ((bf16[128,32,512]{2,1,0:T(8,128)(2,1)}), bf16[128,32,512]{2,1,0:T(8,128)(2,1)}, u32[]{:S(2)}, u32[]{:S(2)}) async-start(bf16[128,32,512]{2,1,0:T(8,128)(2,1)} %copy-done), calls=%async_computation | async-start | bytes 8388608 | tf_op jit(solution)/shard_map/all_to_all | solution.py:17
  40.1 3.5 %collective-permute-start = (bf16[64,56,128]{2,1,0:T(8,128)(2,1)S(1)}, bf16[64,56,128]{2,1,0:T(8,128)(2,1)S(1)}, u32[]{:S(2)}, u32[]{:S(2)}) collective-permute-start(bf16[64,56,128]{2,1,0:T(8,128)(2,1)S(1)} %get-tuple-element.8), channel_id=1, source_target_pairs={{0,1},{1,0},{2,3},{3,2},{4,5},{5,4},{6,7},{7,6},{8,9},{9,8},{10,11... | collective-permute-start | bytes 2752520 | tf_op jit(solution)/shard_map/ppermute | solution.py:249
where the time goes:
time: 118 us; the launch traced here: 117 us
  waiting for transfers between devices  29.7 us (25%)
  local copies, waits for them, and re-layouts  22.5 us (19%)
  Pallas kernels  20.6 us (17%)
  starting transfers between devices  20.5 us (17%)
  blocking collectives  17.9 us (15%)
  matrix products  4.58 us (4%)
    all_to_all x2, waiting for transfers between devices, exchange(): return lax.all_to_all(x, axes, split_axis=0, concat_axis=0, tiled=True)  27.6 us
    all_to_all x2, starting transfers between devices, exchange(): return lax.all_to_all(x, axes, split_axis=0, concat_axis=0, tiled=True)  19.1 us
    all_to_all x1, blocking collectives, exchange(): return lax.all_to_all(x, axes, split_axis=0, concat_axis=0, tiled=True)  17.9 us
    pallas_call x1, Pallas kernels, form_products(): pl.pallas_call(functools.partial(products_kernel, n_down, n_across), grid...  11.9 us
    transpose x1, local copies, waits for them, and re-layouts, per_device(): jnp.einsum('glrp,gsmp->lsrm', early[:, :, :rows], early[:, :, rows:rows +...  9.03 us
    reshape x1, local copies, waits for them, and re-layouts, per_device(): grid = jnp.einsum('glrp,gsmp->lsrm', early[:, :, :rows], early[:, :, rows...  7.34 us
    pallas_call x1, Pallas kernels, sum_by_target(): pl.pallas_call(sum_kernel, grid=(contribs // block,), in_specs=[pl.BlockS...  5.11 us
    dot_general x1, matrix products, per_device(): jnp.einsum('glrp,gsmp->lsrm', early[:, :, :rows], early[:, :, rows:rows +...  4.58 us
  transfers between devices with their start and end apart: 3, of which 3 were waited for; matrix products, arithmetic and copies ran while one was open for 22% of the time, Pallas kernels for 10%

commit v1 on v0

--- a/solution.py
+++ b/solution.py
@@ -21,13 +21,12 @@
     return (i // 2) * (2 * n_across) + 2 * j + i % 2
 
 
-def swap_matrix(per):
-    cols = LANES // per
-    width = per * LANES
-    source = lax.broadcasted_iota(jnp.int32, (width, width), 0)
-    dest = lax.broadcasted_iota(jnp.int32, (width, width), 1)
-    swapped = (dest // cols % per) * LANES + dest // LANES * cols + dest % cols
-    return (source == swapped).astype(jnp.bfloat16)
+def pick_lanes(parts, shift, per):
+    group = lax.broadcasted_iota(jnp.int32, parts[0].shape, 1) // (LANES // per)
+    result = parts[0]
+    for n in range(1, per):
+        result = jnp.where(group == (shift + n) % per, parts[n], result)
+    return result
 
 
 def early_kernel(n_down, n_across, owner_hbm, slot_hbm, front_hbm, panel_hbm, out_ref,
@@ -81,7 +80,7 @@
     )(owner, slot, front, panel)
 
 
-def products_kernel(n_down, n_across, a_ref, scale_ref, swap_ref, out_ref, held_ref):
+def products_kernel(n_down, n_across, a_ref, scale_ref, out_ref, held_ref):
     count, blocks, _, tile, _ = a_ref.shape
     rows, cols = tile // n_down, tile // n_across
     per = LANES // cols
@@ -101,30 +100,22 @@
 
     @pl.when(step == pl.num_programs(1) - 1)
     def _():
-        together = 4
-
-        @pl.loop(0, n_down // together)
-        def _(block):
-            at = [(d, q, h) for d in range(together) for q in range(quads) for h in range(sides)]
-            parts = []
-            for d, q, h in at:
-                row = ((block * together + d) * rows + q * per) * BATCH
-                parts.append(jnp.concatenate([
-                    held_ref[h, pl.ds(pl.multiple_of(row + r * BATCH, BATCH), BATCH), :].astype(jnp.bfloat16)
-                    for r in range(per)
-                ], axis=1))
-            swapped = jnp.dot(
-                jnp.concatenate(parts, axis=0), swap_ref[...], preferred_element_type=jnp.float32
-            ).astype(jnp.bfloat16)
-            for n, (d, q, h) in enumerate(at):
-                for j in range(per):
-                    first = block * (together * n_across) + device_of(d, h * per + j, n_across)
-                    out_ref[first, :, q * LANES:(q + 1) * LANES] = (
-                        swapped[n * BATCH:(n + 1) * BATCH, j * LANES:(j + 1) * LANES]
-                    )
-
-
-def form_products(a_tiles, scaling, swap, n_down, n_across):
+        @pl.loop(0, n_down // 2)
+        def _(pair):
+            for d in range(2):
+                for q in range(quads):
+                    for h in range(sides):
+                        parts = []
+                        for r in range(per):
+                            row = ((pair * 2 + d) * rows + q * per + r) * BATCH
+                            part = held_ref[h, pl.ds(pl.multiple_of(row, BATCH), BATCH), :]
+                            parts.append(pltpu.roll(part, cols * r, axis=1) if r else part)
+                        for j in range(per):
+                            first = pair * (2 * n_across) + device_of(d, h * per + j, n_across)
+                            out_ref[first, :, q * LANES:(q + 1) * LANES] = pick_lanes(parts, j, per).astype(jnp.bfloat16)
+
+
+def form_products(a_tiles, scaling, n_down, n_across):
     contribs, blocks, _, tile, _ = a_tiles.shape
     n_all = n_down * n_across
     chunk = tile * tile // n_all
@@ -136,93 +127,71 @@
         in_specs=[
             pl.BlockSpec((count, blocks, 2, tile, tile), lambda g, s: (g * steps + s, 0, 0, 0, 0)),
             pl.BlockSpec((count, blocks, tile), lambda g, s: (g * steps + s, 0, 0)),
-            pl.BlockSpec(swap.shape, lambda g, s: (0, 0)),
         ],
         out_specs=pl.BlockSpec((n_all, BATCH, chunk), lambda g, s: (0, g, 0)),
         out_shape=jax.ShapeDtypeStruct((n_all, contribs, chunk), jnp.bfloat16),
         scratch_shapes=[pltpu.VMEM((tile // LANES, tile * BATCH, LANES), jnp.float32)],
-        compiler_params=VMEM,
-    )(a_tiles, scaling, swap)
-
-
-def sum_kernel(x_ref, target_ref, update_ref, out_ref, total_ref, spread_ref):
-    step = pl.program_id(0)
-    n_tiles, chunk = total_ref.shape
+        compiler_params=pltpu.CompilerParams(vmem_limit_bytes=64 << 20),
+    )(a_tiles, scaling)
+
+
+def sum_kernel(x_ref, target_ref, update_ref, out_ref, spread_ref):
+    n_tiles, chunk = update_ref.shape
     number = lax.broadcasted_iota(jnp.int32, (n_tiles, x_ref.shape[0]), 0)
-    picking = (number == target_ref[...]).astype(jnp.float32).astype(jnp.bfloat16)
-    part = jnp.dot(picking, x_ref[...], preferred_element_type=jnp.float32)
-
-    @pl.when(step == 0)
-    def _():
-        total_ref[...] = part - update_ref[...]
-
-    @pl.when(step > 0)
-    def _():
-        total_ref[...] += part
-
-    @pl.when(step == pl.num_programs(0) - 1)
-    def _():
-        pieces = chunk // LANES
-        for q in range(pieces):
-            spread_ref[pl.ds(q, n_tiles, stride=pieces), :] = total_ref[:, q * LANES:(q + 1) * LANES]
-        out_ref[...] = spread_ref[...].astype(jnp.bfloat16)
+    picking = jnp.where(number == target_ref[...], 1.0, 0.0).astype(jnp.bfloat16)
+    total = jnp.dot(picking, x_ref[...], preferred_element_type=jnp.float32) - update_ref[...]
+    pieces = chunk // LANES
+    for q in range(pieces):
+        spread_ref[pl.ds(q, n_tiles, stride=pieces), :] = total[:, q * LANES:(q + 1) * LANES]
+    out_ref[...] = spread_ref[...].astype(jnp.bfloat16)
 
 
 def sum_by_target(x, target, update):
     contribs, chunk = x.shape
     n_tiles = update.shape[0]
-    block = 1024
+    vmem = pl.BlockSpec(memory_space=pltpu.VMEM)
     return pl.pallas_call(
         sum_kernel,
-        grid=(contribs // block,),
-        in_specs=[
-            pl.BlockSpec((block, chunk), lambda s: (s, 0)),
-            pl.BlockSpec((1, block), lambda s: (0, s)),
-            pl.BlockSpec((n_tiles, chunk), lambda s: (0, 0)),
-        ],
-        out_specs=pl.BlockSpec((n_tiles * chunk // LANES, LANES), lambda s: (0, 0)),
+        in_specs=[vmem, vmem, vmem],
+        out_specs=vmem,
         out_shape=jax.ShapeDtypeStruct((n_tiles * chunk // LANES, LANES), jnp.bfloat16),
-        scratch_shapes=[
-            pltpu.VMEM((n_tiles, chunk), jnp.float32),
-            pltpu.VMEM((n_tiles * chunk // LANES, LANES), jnp.float32),
-        ],
+        scratch_shapes=[pltpu.VMEM((n_tiles * chunk // LANES, LANES), jnp.float32)],
         compiler_params=VMEM,
     )(x, target.reshape(1, -1), update)
 
 
-def final_kernel(n_down, n_across, x_ref, swap_ref, out_ref, spread_ref):
+def final_kernel(n_down, n_across, x_ref, out_ref, spread_ref):
     held, tile, _ = out_ref.shape
     rows, cols = tile // n_down, tile // n_across
     per = LANES // cols
     quads = rows // per
     sides = tile // LANES
-    at = [(i, h) for i in range(n_down) for h in range(sides)]
-    parts = []
-    for i, h in at:
-        parts.append(jnp.concatenate([x_ref[device_of(i, h * per + j, n_across)] for j in range(per)], axis=1))
-    swapped = jnp.dot(jnp.concatenate(parts, axis=0), swap_ref[...], preferred_element_type=jnp.float32)
-    for n, (i, h) in enumerate(at):
-        for r in range(per):
-            for s in range(held):
-                top = n * held * quads + s * quads
-                spread_ref[h, pl.ds(s * tile + i * rows + r, quads, stride=per), :] = (
-                    swapped[top:top + quads, r * LANES:(r + 1) * LANES]
-                )
+    for i in range(n_down):
+        for h in range(sides):
+            parts = [x_ref[device_of(i, h * per + j, n_across)].astype(jnp.float32) for j in range(per)]
+            for r in range(per):
+                picked = pick_lanes(parts, r, per)
+                if r:
+                    picked = pltpu.roll(picked, LANES - cols * r, axis=1)
+                for s in range(held):
+                    spread_ref[h, pl.ds(s * tile + i * rows + r, quads, stride=per), :] = (
+                        picked[s * quads:(s + 1) * quads]
+                    )
     for s in range(held):
         for h in range(sides):
             out_ref[s, :, h * LANES:(h + 1) * LANES] = spread_ref[h, s * tile:(s + 1) * tile, :]
 
 
-def final_tiles(x, swap, tile, held, n_down, n_across):
+def final_tiles(x, tile, held, n_down, n_across):
     vmem = pl.BlockSpec(memory_space=pltpu.VMEM)
     return pl.pallas_call(
         functools.partial(final_kernel, n_down, n_across),
-        in_specs=[vmem, vmem],
+        in_specs=[vmem],
         out_specs=vmem,
         out_shape=jax.ShapeDtypeStruct((held, tile, tile), jnp.float32),
         scratch_shapes=[pltpu.VMEM((tile // LANES, held * tile, LANES), jnp.float32)],
         compiler_params=VMEM,
-    )(x, swap)
+    )(x)
 
 
 def per_device(a_tiles, scaling, dest_owner, dest_slot, panel, front_tiles):
@@ -237,10 +206,9 @@
     rows, cols = tile // n_down, tile // n_across
     chunk = rows * cols
     depth = panel.shape[1]
-    swap = swap_matrix(LANES // cols)
 
     early = exchange(early_blocks(dest_owner[:, 0], dest_slot, front_tiles, panel, n_down, n_across), PLANE)
-    arrived = exchange(form_products(a_tiles, scaling, swap, n_down, n_across), AXES)
+    arrived = exchange(form_products(a_tiles, scaling, n_down, n_across), AXES)
 
     even = lax.axis_index("core") == 0
     low, high, rest = early[:, :rows], early[:, rows:2 * rows], early[:, 2 * rows:]
@@ -257,14 +225,18 @@
     row_piece = numbers[:, first:first + held].reshape(-1)
     col_piece = numbers[:, first + held:first + 2 * held].reshape(-1)
 
+    per = LANES // cols
+    chip = lax.axis_index("group") * n_chip + lax.axis_index("chip")
+    left = early[:, :, :rows].reshape(n_group, n_dev, rows // per, per, depth)
+    left = jnp.roll(left, chip % per, axis=3).reshape(n_group, n_dev, rows, depth)
     grid = jnp.einsum(
-        "glrp,gsmp->lsrm", early[:, :, :rows], early[:, :, rows:rows + cols], preferred_element_type=jnp.float32
+        "glrp,gsmp->lsrm", left, early[:, :, rows:rows + cols], preferred_element_type=jnp.float32
     ).reshape(n_dev * n_dev, chunk)
     update = jnp.take(grid, row_piece * n_dev + col_piece, axis=0, mode="clip")
 
     sums = sum_by_target(arrived.reshape(n_all * contribs, chunk), target, update)
     final = exchange(sums.reshape(n_all, held * chunk // LANES, LANES), AXES)
-    return final_tiles(final, swap, tile, held, n_down, n_across)
+    return final_tiles(final, tile, held, n_down, n_across)
 
 
 def solution(mesh):

time: 118 us -> 117 us (level)
  local copies, waits for them, and re-layouts: 22.5 us -> 19.5 us
  other arithmetic: 1.09 us -> 3.11 us
    gather x1, local copies, waits for them, and re-layouts: 3.62 us -> 1.62 us  [per_device(): update = jnp.take(grid, row_piece * n_dev + col_piece, axis=0, mode='clip')]
    reshape x1 -> x2, local copies, waits for them, and re-layouts: 7.34 us -> 6.38 us  [the longest x1 6.24 us: per_device(): grid = jnp.einsum('glrp,gsmp->lsrm', left, early[:, :, rows:rows + cols],...]
  transfers between devices with their start and end apart: 3 -> 3, of which waited for: 3 -> 3; matrix products, arithmetic and copies ran while one was open for 22% -> 23% of each run, Pallas kernels for 10% -> 11%
where the time goes in v1:
time: 117 us; the launch traced here: 116 us
  waiting for transfers between devices  29.8 us (25%)
  Pallas kernels  20.7 us (18%)
  starting transfers between devices  20.6 us (18%)
  local copies, waits for them, and re-layouts  19.5 us (17%)
  blocking collectives  17.9 us (15%)
  matrix products  4.6 us (4%)
  other arithmetic  3.11 us (3%)
    all_to_all x2, waiting for transfers between devices, exchange(): return lax.all_to_all(x, axes, split_axis=0, concat_axis=0, tiled=True)  27.7 us
    all_to_all x2, starting transfers between devices, exchange(): return lax.all_to_all(x, axes, split_axis=0, concat_axis=0, tiled=True)  19.2 us
    all_to_all x1, blocking collectives, exchange(): return lax.all_to_all(x, axes, split_axis=0, concat_axis=0, tiled=True)  17.9 us
    pallas_call x1, Pallas kernels, form_products(): pl.pallas_call(functools.partial(products_kernel, n_down, n_across), grid...  12.7 us
    transpose x1, local copies, waits for them, and re-layouts, per_device(): jnp.einsum('glrp,gsmp->lsrm', left, early[:, :, rows:rows + cols], prefer...  9.03 us
    reshape x1, local copies, waits for them, and re-layouts, per_device(): grid = jnp.einsum('glrp,gsmp->lsrm', left, early[:, :, rows:rows + cols],...  6.24 us
    dot_general x1, matrix products, per_device(): jnp.einsum('glrp,gsmp->lsrm', left, early[:, :, rows:rows + cols], prefer...  4.6 us
    pallas_call x1, Pallas kernels, sum_by_target(): pl.pallas_call(sum_kernel, in_specs=[vmem, vmem, vmem], out_specs=vmem, o...  4.56 us
  transfers between devices with their start and end apart: 3, of which 3 were waited for; matrix products, arithmetic and copies ran while one was open for 23% of the time, Pallas kernels for 11%

profile of v1, /device:TPU:1, one launch (start us, length us, event | category | flops | bytes accessed | tf_op | source)
XLA Modules:
  0.0 116.3 jit_solution(4285602637889262105)
XLA Ops:
  0.0 2.1 %shard_map.65 = bf16[64,72,128]{2,1,0:T(8,128)(2,1)} custom-call(s32[32]{0:T(128)} %bitcast.36, s32[32]{0:T(128)} %slot_hbm.1, s32[2,4]{1,0:T(2,128)} %bitcast.35, bf16[256,128]{1,0:T(8,128)(2,1)} %panel_hbm.1), custom_call_target="tpu_custom_call" | custom-call | tf_op jit(solution)/shard_map/pallas_call | solution.py:67
  2.1 12.2 %all-to-all-start.1 = ((bf16[64,72,128]{2,1,0:T(8,128)(2,1)}), bf16[64,72,128]{2,1,0:T(8,128)(2,1)}, u32[]{:S(2)}, u32[]{:S(2)}) async-start(bf16[64,72,128]{2,1,0:T(8,128)(2,1)} %shard_map.65), calls=%async_computation.1 | async-start | bytes 2359296 | tf_op jit(solution)/shard_map/all_to_all | solution.py:17
  14.3 12.7 %shard_map.64 = bf16[128,32,512]{2,1,0:T(8,128)(2,1)} custom-call(bf16[32,2,2,256,256]{4,3,2,1,0:T(8,128)(2,1)} %a_ref.1, f32[32,2,256]{2,1,0:T(2,128)} %scale_ref.1), custom_call_target="tpu_custom_call" | custom-call | tf_op jit(solution)/shard_map/pallas_call | solution.py:124
  27.0 5.7 %all-to-all-done.1 = bf16[64,72,128]{2,1,0:T(8,128)(2,1)} async-done(((bf16[64,72,128]{2,1,0:T(8,128)(2,1)}), bf16[64,72,128]{2,1,0:T(8,128)(2,1)}, u32[]{:S(2)}, u32[]{:S(2)}) %all-to-all-start.1) | async-done | bytes 1179680 | tf_op jit(solution)/shard_map/all_to_all | solution.py:17
  32.7 7.0 %all-to-all-start = ((bf16[128,32,512]{2,1,0:T(8,128)(2,1)}), bf16[128,32,512]{2,1,0:T(8,128)(2,1)}, u32[]{:S(2)}, u32[]{:S(2)}) async-start(bf16[128,32,512]{2,1,0:T(8,128)(2,1)} %shard_map.64), calls=%async_computation | async-start | bytes 8388608 | tf_op jit(solution)/shard_map/all_to_all | solution.py:17
  39.8 1.2 slice.44
  40.9 1.1 broadcast_select_fusion.1
  42.0 0.2 fusion
  42.2 1.4 %collective-permute-start = (bf16[64,56,128]{2,1,0:T(8,128)(2,1)S(1)}, bf16[64,56,128]{2,1,0:T(8,128)(2,1)S(1)}, u32[]{:S(2)}, u32[]{:S(2)}) collective-permute-start(bf16[64,56,128]{2,1,0:T(8,128)(2,1)S(1)} %get-tuple-element.8), channel_id=1, source_target_pairs={{0,1},{1,0},{2,3},{3,2},{4,5},{5,4},{6,7},{7,6},{8,9},{9,8},{10,11... | collective-permute-start | bytes 2752520 | tf_op jit(solution)/shard_map/ppermute | solution.py:217
  43.6 2.1 %collective-permute-done = bf16[64,56,128]{2,1,0:T(8,128)(2,1)S(1)} collective-permute-done((bf16[64,56,128]{2,1,0:T(8,128)(2,1)S(1)}, bf16[64,56,128]{2,1,0:T(8,128)(2,1)S(1)}, u32[]{:S(2)}, u32[]{:S(2)}) %collective-permute-start) | collective-permute-done | bytes 917536 | tf_op jit(solution)/shard_map/ppermute | solution.py:217
  45.7 0.3 maximum_select_fusion
  46.0 0.1 copy.9
  46.2 0.0 copy-start
  46.2 0.1 copy.11
  46.3 0.2 fusion.1
  46.6 0.9 copy-done
  47.4 4.6 %convolution_bitcast_fusion = f32[32,32,16,32]{0,3,2,1:T(8,128)} fusion(bf16[4,32,16,128,1]{3,1,0,2,4:T(8,128)(2,1)S(1)} %bitcast.34, bf16[4,32,56,128]{3,2,1,0:T(8,128)(2,1)S(1)} %bitcast.28), kind=kOutput, calls=%fused_computation.1 | convolution fusion | flops 536870912 | bytes 3670016 | tf_op jit(solution)/shard_map/glrp,gsmp->lsrm/dot_general | solution.py:232
  52.0 9.0 %copy.13 = f32[32,32,16,32]{3,2,1,0:T(8,128)} copy(f32[32,32,16,32]{0,3,2,1:T(8,128)} %convolution_bitcast_fusion) | data formatting | bytes 4194304 | tf_op jit(solution)/shard_map/glrp,gsmp->lsrm/transpose | solution.py:232
  61.1 6.2 %reshape.174 = f32[1024,512]{1,0:T(8,128)S(1)} reshape(f32[32,32,16,32]{3,2,1,0:T(8,128)} %copy.13) | data formatting | bytes 4194304 | tf_op jit(solution)/shard_map/reshape | solution.py:234
  67.3 1.0 slice_convert_fusion
  68.3 0.1 slice_add_fusion
  68.4 0.1 reshape.179
  68.5 0.1 fusion.3
  68.6 0.1 mul.47
  68.7 0.1 reshape.171
  68.8 1.6 %gather_fusion = f32[512,512]{1,0:T(8,128)S(1)} fusion(f32[1024,512]{1,0:T(8,128)S(1)} %reshape.174, s32[1024]{0:T(1024)S(1)} %pad_clamp_fusion), kind=kCustom, calls=%fused_computation | custom fusion | bytes 2099200 | tf_op jit(solution)/shard_map/jit(_take)/gather | solution.py:235
  70.5 0.1 fusion.2.target_ref
  70.6 21.9 %all-to-all-done = bf16[128,32,512]{2,1,0:T(8,128)(2,1)} async-done(((bf16[128,32,512]{2,1,0:T(8,128)(2,1)}), bf16[128,32,512]{2,1,0:T(8,128)(2,1)}, u32[]{:S(2)}, u32[]{:S(2)}) %all-to-all-start) | async-done | bytes 4194336 | tf_op jit(solution)/shard_map/all_to_all | solution.py:17
  92.5 4.6 %shard_map.66 = bf16[2048,128]{1,0:T(8,128)(2,1)S(1)} custom-call(bf16[4096,512]{1,0:T(8,128)(2,1)} %bitcast.x_ref, s32[1,4096]{1,0:T(1,128)S(1)} %fusion.2.target_ref, f32[512,512]{1,0:T(8,128)S(1)} %gather_fusion), custom_call_target="tpu_custom_call" | custom-call | tf_op jit(solution)/shard_map/pallas_call | solution.py:153
  97.1 17.9 %all_to_all.15.x_ref = bf16[128,16,128]{2,1,0:T(8,128)(2,1)S(1)} all-to-all(bf16[128,16,128]{2,1,0:T(8,128)(2,1)S(1)} %bitcast.26), channel_id=1, replica_groups=mesh['group'=4,'chip'=16,'core'=2] {'group','chip','core'}, dimensions={0} | all-to-all | bytes 1048576 | tf_op jit(solution)/shard_map/all_to_all | solution.py:17
  115.0 1.3 %shard_map.67 = f32[4,256,256]{2,1,0:T(8,128)} custom-call(bf16[128,16,128]{2,1,0:T(8,128)(2,1)S(1)} %all_to_all.15.x_ref), custom_call_target="tpu_custom_call" | custom-call | tf_op jit(solution)/shard_map/pallas_call | solution.py:187
  (2 shorter events, 0.0 us)
Async XLA Ops:
  2.1 30.6 %all-to-all-start.1 = ((bf16[64,72,128]{2,1,0:T(8,128)(2,1)}), bf16[64,72,128]{2,1,0:T(8,128)(2,1)}, u32[]{:S(2)}, u32[]{:S(2)}) async-start(bf16[64,72,128]{2,1,0:T(8,128)(2,1)} %shard_map.65), calls=%async_computation.1 | async-start | bytes 2359296 | tf_op jit(solution)/shard_map/all_to_all | solution.py:17
  32.7 59.8 %all-to-all-start = ((bf16[128,32,512]{2,1,0:T(8,128)(2,1)}), bf16[128,32,512]{2,1,0:T(8,128)(2,1)}, u32[]{:S(2)}, u32[]{:S(2)}) async-start(bf16[128,32,512]{2,1,0:T(8,128)(2,1)} %shard_map.64), calls=%async_computation | async-start | bytes 8388608 | tf_op jit(solution)/shard_map/all_to_all | solution.py:17
  42.2 3.5 %collective-permute-start = (bf16[64,56,128]{2,1,0:T(8,128)(2,1)S(1)}, bf16[64,56,128]{2,1,0:T(8,128)(2,1)S(1)}, u32[]{:S(2)}, u32[]{:S(2)}) collective-permute-start(bf16[64,56,128]{2,1,0:T(8,128)(2,1)S(1)} %get-tuple-element.8), channel_id=1, source_target_pairs={{0,1},{1,0},{2,3},{3,2},{4,5},{5,4},{6,7},{7,6},{8,9},{9,8},{10,11... | collective-permute-start | bytes 2752520 | tf_op jit(solution)/shard_map/ppermute | solution.py:217
  46.2 1.3 %copy-start = (bf16[64,2,56,128]{3,2,1,0:T(8,128)(2,1)}, bf16[64,2,56,128]{3,2,1,0:T(8,128)(2,1)S(1)}, u32[]{:S(2)}) copy-start(bf16[64,2,56,128]{3,2,1,0:T(8,128)(2,1)S(1)} %copy.9) | copy-start | bytes 5505028

commit v2 on v1

--- a/solution.py
+++ b/solution.py
@@ -135,11 +135,22 @@
     )(a_tiles, scaling)
 
 
-def sum_kernel(x_ref, target_ref, update_ref, out_ref, spread_ref):
+def sum_kernel(x_hbm, target_ref, update_ref, out_ref, x_ref, spread_ref, sem_ref):
     n_tiles, chunk = update_ref.shape
-    number = lax.broadcasted_iota(jnp.int32, (n_tiles, x_ref.shape[0]), 0)
-    picking = jnp.where(number == target_ref[...], 1.0, 0.0).astype(jnp.bfloat16)
-    total = jnp.dot(picking, x_ref[...], preferred_element_type=jnp.float32) - update_ref[...]
+    parts = sem_ref.shape[0]
+    share = x_ref.shape[0] // parts
+    copies = []
+    for n in range(parts):
+        at = pl.ds(n * share, share)
+        copies.append(pltpu.make_async_copy(x_hbm.at[at], x_ref.at[at], sem_ref.at[n]))
+        copies[n].start()
+    number = lax.broadcasted_iota(jnp.int32, (n_tiles, share), 0)
+    total = -update_ref[...]
+    for n in range(parts):
+        at = slice(n * share, (n + 1) * share)
+        picking = jnp.where(number == target_ref[:, at], 1.0, 0.0).astype(jnp.bfloat16)
+        copies[n].wait()
+        total += jnp.dot(picking, x_ref[at, :], preferred_element_type=jnp.float32)
     pieces = chunk // LANES
     for q in range(pieces):
         spread_ref[pl.ds(q, n_tiles, stride=pieces), :] = total[:, q * LANES:(q + 1) * LANES]
@@ -147,15 +158,18 @@
 
 
 def sum_by_target(x, target, update):
-    contribs, chunk = x.shape
-    n_tiles = update.shape[0]
+    n_tiles, chunk = update.shape
     vmem = pl.BlockSpec(memory_space=pltpu.VMEM)
     return pl.pallas_call(
         sum_kernel,
-        in_specs=[vmem, vmem, vmem],
+        in_specs=[pl.BlockSpec(memory_space=pltpu.HBM), vmem, vmem],
         out_specs=vmem,
         out_shape=jax.ShapeDtypeStruct((n_tiles * chunk // LANES, LANES), jnp.bfloat16),
-        scratch_shapes=[pltpu.VMEM((n_tiles * chunk // LANES, LANES), jnp.float32)],
+        scratch_shapes=[
+            pltpu.VMEM(x.shape, x.dtype),
+            pltpu.VMEM((n_tiles * chunk // LANES, LANES), jnp.float32),
+            pltpu.SemaphoreType.DMA((4,)),
+        ],
         compiler_params=VMEM,
     )(x, target.reshape(1, -1), update)
 

time: 117 us -> 117 us (level)
  no operation moved by 1% of the time
where the time goes in v2:
time: 117 us; the launch traced here: 116 us
  waiting for transfers between devices  29.8 us (25%)
  starting transfers between devices  20.6 us (18%)
  Pallas kernels  20.5 us (18%)
  local copies, waits for them, and re-layouts  19.5 us (17%)
  blocking collectives  17.9 us (15%)
  matrix products  4.6 us (4%)
  other arithmetic  3.11 us (3%)
    all_to_all x2, waiting for transfers between devices, exchange(): return lax.all_to_all(x, axes, split_axis=0, concat_axis=0, tiled=True)  27.7 us
    all_to_all x2, starting transfers between devices, exchange(): return lax.all_to_all(x, axes, split_axis=0, concat_axis=0, tiled=True)  19.2 us
    all_to_all x1, blocking collectives, exchange(): return lax.all_to_all(x, axes, split_axis=0, concat_axis=0, tiled=True)  17.9 us
    pallas_call x1, Pallas kernels, form_products(): pl.pallas_call(functools.partial(products_kernel, n_down, n_across), grid...  12.7 us
    transpose x1, local copies, waits for them, and re-layouts, per_device(): jnp.einsum('glrp,gsmp->lsrm', left, early[:, :, rows:rows + cols], prefer...  9.03 us
    reshape x1, local copies, waits for them, and re-layouts, per_device(): grid = jnp.einsum('glrp,gsmp->lsrm', left, early[:, :, rows:rows + cols],...  6.24 us
    dot_general x1, matrix products, per_device(): jnp.einsum('glrp,gsmp->lsrm', left, early[:, :, rows:rows + cols], prefer...  4.6 us
    pallas_call x1, Pallas kernels, sum_by_target(): pl.pallas_call(sum_kernel, in_specs=[pl.BlockSpec(memory_space=pltpu.HBM)...  4.4 us
  transfers between devices with their start and end apart: 3, of which 3 were waited for; matrix products, arithmetic and copies ran while one was open for 23% of the time, Pallas kernels for 11%

profile of v2, /device:TPU:1, one launch (start us, length us, event | category | flops | bytes accessed | tf_op | source)
XLA Modules:
  0.0 116.1 jit_solution(212181452867048014)
XLA Ops:
  0.0 2.1 %shard_map.65 = bf16[64,72,128]{2,1,0:T(8,128)(2,1)} custom-call(s32[32]{0:T(128)} %bitcast.36, s32[32]{0:T(128)} %slot_hbm.1, s32[2,4]{1,0:T(2,128)} %bitcast.35, bf16[256,128]{1,0:T(8,128)(2,1)} %panel_hbm.1), custom_call_target="tpu_custom_call" | custom-call | tf_op jit(solution)/shard_map/pallas_call | solution.py:67
  2.1 12.2 %all-to-all-start.1 = ((bf16[64,72,128]{2,1,0:T(8,128)(2,1)}), bf16[64,72,128]{2,1,0:T(8,128)(2,1)}, u32[]{:S(2)}, u32[]{:S(2)}) async-start(bf16[64,72,128]{2,1,0:T(8,128)(2,1)} %shard_map.65), calls=%async_computation.1 | async-start | bytes 2359296 | tf_op jit(solution)/shard_map/all_to_all | solution.py:17
  14.3 12.7 %shard_map.64 = bf16[128,32,512]{2,1,0:T(8,128)(2,1)} custom-call(bf16[32,2,2,256,256]{4,3,2,1,0:T(8,128)(2,1)} %a_ref.1, f32[32,2,256]{2,1,0:T(2,128)} %scale_ref.1), custom_call_target="tpu_custom_call" | custom-call | tf_op jit(solution)/shard_map/pallas_call | solution.py:124
  27.0 5.7 %all-to-all-done.1 = bf16[64,72,128]{2,1,0:T(8,128)(2,1)} async-done(((bf16[64,72,128]{2,1,0:T(8,128)(2,1)}), bf16[64,72,128]{2,1,0:T(8,128)(2,1)}, u32[]{:S(2)}, u32[]{:S(2)}) %all-to-all-start.1) | async-done | bytes 1179680 | tf_op jit(solution)/shard_map/all_to_all | solution.py:17
  32.7 7.0 %all-to-all-start = ((bf16[128,32,512]{2,1,0:T(8,128)(2,1)}), bf16[128,32,512]{2,1,0:T(8,128)(2,1)}, u32[]{:S(2)}, u32[]{:S(2)}) async-start(bf16[128,32,512]{2,1,0:T(8,128)(2,1)} %shard_map.64), calls=%async_computation | async-start | bytes 8388608 | tf_op jit(solution)/shard_map/all_to_all | solution.py:17
  39.8 1.2 slice.44
  40.9 1.1 broadcast_select_fusion.1
  42.0 0.2 fusion
  42.2 1.4 %collective-permute-start = (bf16[64,56,128]{2,1,0:T(8,128)(2,1)S(1)}, bf16[64,56,128]{2,1,0:T(8,128)(2,1)S(1)}, u32[]{:S(2)}, u32[]{:S(2)}) collective-permute-start(bf16[64,56,128]{2,1,0:T(8,128)(2,1)S(1)} %get-tuple-element.8), channel_id=1, source_target_pairs={{0,1},{1,0},{2,3},{3,2},{4,5},{5,4},{6,7},{7,6},{8,9},{9,8},{10,11... | collective-permute-start | bytes 2752520 | tf_op jit(solution)/shard_map/ppermute | solution.py:231
  43.6 2.1 %collective-permute-done = bf16[64,56,128]{2,1,0:T(8,128)(2,1)S(1)} collective-permute-done((bf16[64,56,128]{2,1,0:T(8,128)(2,1)S(1)}, bf16[64,56,128]{2,1,0:T(8,128)(2,1)S(1)}, u32[]{:S(2)}, u32[]{:S(2)}) %collective-permute-start) | collective-permute-done | bytes 917536 | tf_op jit(solution)/shard_map/ppermute | solution.py:231
  45.7 0.3 maximum_select_fusion
  46.0 0.1 copy.9
  46.2 0.0 copy-start
  46.2 0.1 copy.11
  46.3 0.2 fusion.1
  46.6 0.9 copy-done
  47.4 4.6 %convolution_bitcast_fusion = f32[32,32,16,32]{0,3,2,1:T(8,128)} fusion(bf16[4,32,16,128,1]{3,1,0,2,4:T(8,128)(2,1)S(1)} %bitcast.34, bf16[4,32,56,128]{3,2,1,0:T(8,128)(2,1)S(1)} %bitcast.28), kind=kOutput, calls=%fused_computation.1 | convolution fusion | flops 536870912 | bytes 3670016 | tf_op jit(solution)/shard_map/glrp,gsmp->lsrm/dot_general | solution.py:246
  52.0 9.0 %copy.13 = f32[32,32,16,32]{3,2,1,0:T(8,128)} copy(f32[32,32,16,32]{0,3,2,1:T(8,128)} %convolution_bitcast_fusion) | data formatting | bytes 4194304 | tf_op jit(solution)/shard_map/glrp,gsmp->lsrm/transpose | solution.py:246
  61.1 6.2 %reshape.174 = f32[1024,512]{1,0:T(8,128)S(1)} reshape(f32[32,32,16,32]{3,2,1,0:T(8,128)} %copy.13) | data formatting | bytes 4194304 | tf_op jit(solution)/shard_map/reshape | solution.py:248
  67.3 1.0 slice_convert_fusion
  68.3 0.1 slice_add_fusion
  68.4 0.1 reshape.179
  68.5 0.1 fusion.3
  68.6 0.1 mul.47
  68.7 0.1 reshape.171
  68.8 1.6 %gather_fusion = f32[512,512]{1,0:T(8,128)S(1)} fusion(f32[1024,512]{1,0:T(8,128)S(1)} %reshape.174, s32[1024]{0:T(1024)S(1)} %pad_clamp_fusion), kind=kCustom, calls=%fused_computation | custom fusion | bytes 2099200 | tf_op jit(solution)/shard_map/jit(_take)/gather | solution.py:249
  70.5 0.1 fusion.2.target_ref
  70.6 21.9 %all-to-all-done = bf16[128,32,512]{2,1,0:T(8,128)(2,1)} async-done(((bf16[128,32,512]{2,1,0:T(8,128)(2,1)}), bf16[128,32,512]{2,1,0:T(8,128)(2,1)}, u32[]{:S(2)}, u32[]{:S(2)}) %all-to-all-start) | async-done | bytes 4194336 | tf_op jit(solution)/shard_map/all_to_all | solution.py:17
  92.5 4.4 %shard_map.66 = bf16[2048,128]{1,0:T(8,128)(2,1)S(1)} custom-call(bf16[4096,512]{1,0:T(8,128)(2,1)} %bitcast.x_hbm, s32[1,4096]{1,0:T(1,128)S(1)} %fusion.2.target_ref, f32[512,512]{1,0:T(8,128)S(1)} %gather_fusion), custom_call_target="tpu_custom_call" | custom-call | tf_op jit(solution)/shard_map/pallas_call | solution.py:163
  96.9 17.9 %all_to_all.15.x_ref = bf16[128,16,128]{2,1,0:T(8,128)(2,1)S(1)} all-to-all(bf16[128,16,128]{2,1,0:T(8,128)(2,1)S(1)} %bitcast.26), channel_id=1, replica_groups=mesh['group'=4,'chip'=16,'core'=2] {'group','chip','core'}, dimensions={0} | all-to-all | bytes 1048576 | tf_op jit(solution)/shard_map/all_to_all | solution.py:17
  114.8 1.3 %shard_map.67 = f32[4,256,256]{2,1,0:T(8,128)} custom-call(bf16[128,16,128]{2,1,0:T(8,128)(2,1)S(1)} %all_to_all.15.x_ref), custom_call_target="tpu_custom_call" | custom-call | tf_op jit(solution)/shard_map/pallas_call | solution.py:201
  (2 shorter events, 0.0 us)
Async XLA Ops:
  2.1 30.6 %all-to-all-start.1 = ((bf16[64,72,128]{2,1,0:T(8,128)(2,1)}), bf16[64,72,128]{2,1,0:T(8,128)(2,1)}, u32[]{:S(2)}, u32[]{:S(2)}) async-start(bf16[64,72,128]{2,1,0:T(8,128)(2,1)} %shard_map.65), calls=%async_computation.1 | async-start | bytes 2359296 | tf_op jit(solution)/shard_map/all_to_all | solution.py:17
  32.7 59.8 %all-to-all-start = ((bf16[128,32,512]{2,1,0:T(8,128)(2,1)}), bf16[128,32,512]{2,1,0:T(8,128)(2,1)}, u32[]{:S(2)}, u32[]{:S(2)}) async-start(bf16[128,32,512]{2,1,0:T(8,128)(2,1)} %shard_map.64), calls=%async_computation | async-start | bytes 8388608 | tf_op jit(solution)/shard_map/all_to_all | solution.py:17
  42.2 3.5 %collective-permute-start = (bf16[64,56,128]{2,1,0:T(8,128)(2,1)S(1)}, bf16[64,56,128]{2,1,0:T(8,128)(2,1)S(1)}, u32[]{:S(2)}, u32[]{:S(2)}) collective-permute-start(bf16[64,56,128]{2,1,0:T(8,128)(2,1)S(1)} %get-tuple-element.8), channel_id=1, source_target_pairs={{0,1},{1,0},{2,3},{3,2},{4,5},{5,4},{6,7},{7,6},{8,9},{9,8},{10,11... | collective-permute-start | bytes 2752520 | tf_op jit(solution)/shard_map/ppermute | solution.py:231
  46.2 1.3 %copy-start = (bf16[64,2,56,128]{3,2,1,0:T(8,128)(2,1)}, bf16[64,2,56,128]{3,2,1,0:T(8,128)(2,1)S(1)}, u32[]{:S(2)}) copy-start(bf16[64,2,56,128]{3,2,1,0:T(8,128)(2,1)S(1)} %copy.9) | copy-start | bytes 5505028

commit v3 on v2

--- a/solution.py
+++ b/solution.py
@@ -130,7 +130,7 @@
         ],
         out_specs=pl.BlockSpec((n_all, BATCH, chunk), lambda g, s: (0, g, 0)),
         out_shape=jax.ShapeDtypeStruct((n_all, contribs, chunk), jnp.bfloat16),
-        scratch_shapes=[pltpu.VMEM((tile // LANES, tile * BATCH, LANES), jnp.float32)],
+        scratch_shapes=[pltpu.VMEM((tile // LANES, (tile + 1) * BATCH, LANES), jnp.float32)],
         compiler_params=pltpu.CompilerParams(vmem_limit_bytes=64 << 20),
     )(a_tiles, scaling)
 
@@ -154,7 +154,7 @@
     pieces = chunk // LANES
     for q in range(pieces):
         spread_ref[pl.ds(q, n_tiles, stride=pieces), :] = total[:, q * LANES:(q + 1) * LANES]
-    out_ref[...] = spread_ref[...].astype(jnp.bfloat16)
+    out_ref[...] = spread_ref[0:n_tiles * pieces, :].astype(jnp.bfloat16)
 
 
 def sum_by_target(x, target, update):
@@ -167,7 +167,7 @@
         out_shape=jax.ShapeDtypeStruct((n_tiles * chunk // LANES, LANES), jnp.bfloat16),
         scratch_shapes=[
             pltpu.VMEM(x.shape, x.dtype),
-            pltpu.VMEM((n_tiles * chunk // LANES, LANES), jnp.float32),
+            pltpu.VMEM((n_tiles * chunk // LANES + 8, LANES), jnp.float32),
             pltpu.SemaphoreType.DMA((4,)),
         ],
         compiler_params=VMEM,
@@ -203,7 +203,7 @@
         in_specs=[vmem],
         out_specs=vmem,
         out_shape=jax.ShapeDtypeStruct((held, tile, tile), jnp.float32),
-        scratch_shapes=[pltpu.VMEM((tile // LANES, held * tile, LANES), jnp.float32)],
+        scratch_shapes=[pltpu.VMEM((tile // LANES, held * tile + 8, LANES), jnp.float32)],
         compiler_params=VMEM,
     )(x)
 

time: 117 us -> 117 us (level)
  no operation moved by 1% of the time
where the time goes in v3:
time: 117 us; the launch traced here: 116 us
  waiting for transfers between devices  29.8 us (25%)
  starting transfers between devices  20.6 us (18%)
  Pallas kernels  20.5 us (18%)
  local copies, waits for them, and re-layouts  19.5 us (17%)
  blocking collectives  17.9 us (15%)
  matrix products  4.6 us (4%)
  other arithmetic  3.11 us (3%)
    all_to_all x2, waiting for transfers between devices, exchange(): return lax.all_to_all(x, axes, split_axis=0, concat_axis=0, tiled=True)  27.7 us
    all_to_all x2, starting transfers between devices, exchange(): return lax.all_to_all(x, axes, split_axis=0, concat_axis=0, tiled=True)  19.2 us
    all_to_all x1, blocking collectives, exchange(): return lax.all_to_all(x, axes, split_axis=0, concat_axis=0, tiled=True)  17.9 us
    pallas_call x1, Pallas kernels, form_products(): pl.pallas_call(functools.partial(products_kernel, n_down, n_across), grid...  12.7 us
    transpose x1, local copies, waits for them, and re-layouts, per_device(): jnp.einsum('glrp,gsmp->lsrm', left, early[:, :, rows:rows + cols], prefer...  9.03 us
    reshape x1, local copies, waits for them, and re-layouts, per_device(): grid = jnp.einsum('glrp,gsmp->lsrm', left, early[:, :, rows:rows + cols],...  6.24 us
    dot_general x1, matrix products, per_device(): jnp.einsum('glrp,gsmp->lsrm', left, early[:, :, rows:rows + cols], prefer...  4.6 us
    pallas_call x1, Pallas kernels, sum_by_target(): pl.pallas_call(sum_kernel, in_specs=[pl.BlockSpec(memory_space=pltpu.HBM)...  4.39 us
  transfers between devices with their start and end apart: 3, of which 3 were waited for; matrix products, arithmetic and copies ran while one was open for 23% of the time, Pallas kernels for 11%

profile of v3, /device:TPU:1, one launch (start us, length us, event | category | flops | bytes accessed | tf_op | source)
XLA Modules:
  0.0 116.1 jit_solution(11566670956548268795)
XLA Ops:
  0.0 2.1 %shard_map.65 = bf16[64,72,128]{2,1,0:T(8,128)(2,1)} custom-call(s32[32]{0:T(128)} %bitcast.36, s32[32]{0:T(128)} %slot_hbm.1, s32[2,4]{1,0:T(2,128)} %bitcast.35, bf16[256,128]{1,0:T(8,128)(2,1)} %panel_hbm.1), custom_call_target="tpu_custom_call" | custom-call | tf_op jit(solution)/shard_map/pallas_call | solution.py:67
  2.1 12.2 %all-to-all-start.1 = ((bf16[64,72,128]{2,1,0:T(8,128)(2,1)}), bf16[64,72,128]{2,1,0:T(8,128)(2,1)}, u32[]{:S(2)}, u32[]{:S(2)}) async-start(bf16[64,72,128]{2,1,0:T(8,128)(2,1)} %shard_map.65), calls=%async_computation.1 | async-start | bytes 2359296 | tf_op jit(solution)/shard_map/all_to_all | solution.py:17
  14.3 12.7 %shard_map.64 = bf16[128,32,512]{2,1,0:T(8,128)(2,1)} custom-call(bf16[32,2,2,256,256]{4,3,2,1,0:T(8,128)(2,1)} %a_ref.1, f32[32,2,256]{2,1,0:T(2,128)} %scale_ref.1), custom_call_target="tpu_custom_call" | custom-call | tf_op jit(solution)/shard_map/pallas_call | solution.py:124
  27.0 5.7 %all-to-all-done.1 = bf16[64,72,128]{2,1,0:T(8,128)(2,1)} async-done(((bf16[64,72,128]{2,1,0:T(8,128)(2,1)}), bf16[64,72,128]{2,1,0:T(8,128)(2,1)}, u32[]{:S(2)}, u32[]{:S(2)}) %all-to-all-start.1) | async-done | bytes 1179680 | tf_op jit(solution)/shard_map/all_to_all | solution.py:17
  32.7 7.0 %all-to-all-start = ((bf16[128,32,512]{2,1,0:T(8,128)(2,1)}), bf16[128,32,512]{2,1,0:T(8,128)(2,1)}, u32[]{:S(2)}, u32[]{:S(2)}) async-start(bf16[128,32,512]{2,1,0:T(8,128)(2,1)} %shard_map.64), calls=%async_computation | async-start | bytes 8388608 | tf_op jit(solution)/shard_map/all_to_all | solution.py:17
  39.8 1.2 slice.44
  40.9 1.1 broadcast_select_fusion.1
  42.0 0.2 fusion
  42.2 1.4 %collective-permute-start = (bf16[64,56,128]{2,1,0:T(8,128)(2,1)S(1)}, bf16[64,56,128]{2,1,0:T(8,128)(2,1)S(1)}, u32[]{:S(2)}, u32[]{:S(2)}) collective-permute-start(bf16[64,56,128]{2,1,0:T(8,128)(2,1)S(1)} %get-tuple-element.8), channel_id=1, source_target_pairs={{0,1},{1,0},{2,3},{3,2},{4,5},{5,4},{6,7},{7,6},{8,9},{9,8},{10,11... | collective-permute-start | bytes 2752520 | tf_op jit(solution)/shard_map/ppermute | solution.py:231
  43.6 2.1 %collective-permute-done = bf16[64,56,128]{2,1,0:T(8,128)(2,1)S(1)} collective-permute-done((bf16[64,56,128]{2,1,0:T(8,128)(2,1)S(1)}, bf16[64,56,128]{2,1,0:T(8,128)(2,1)S(1)}, u32[]{:S(2)}, u32[]{:S(2)}) %collective-permute-start) | collective-permute-done | bytes 917536 | tf_op jit(solution)/shard_map/ppermute | solution.py:231
  45.7 0.3 maximum_select_fusion
  46.0 0.1 copy.9
  46.2 0.0 copy-start
  46.2 0.1 copy.11
  46.3 0.2 fusion.1
  46.6 0.9 copy-done
  47.4 4.6 %convolution_bitcast_fusion = f32[32,32,16,32]{0,3,2,1:T(8,128)} fusion(bf16[4,32,16,128,1]{3,1,0,2,4:T(8,128)(2,1)S(1)} %bitcast.34, bf16[4,32,56,128]{3,2,1,0:T(8,128)(2,1)S(1)} %bitcast.28), kind=kOutput, calls=%fused_computation.1 | convolution fusion | flops 536870912 | bytes 3670016 | tf_op jit(solution)/shard_map/glrp,gsmp->lsrm/dot_general | solution.py:246
  52.0 9.0 %copy.13 = f32[32,32,16,32]{3,2,1,0:T(8,128)} copy(f32[32,32,16,32]{0,3,2,1:T(8,128)} %convolution_bitcast_fusion) | data formatting | bytes 4194304 | tf_op jit(solution)/shard_map/glrp,gsmp->lsrm/transpose | solution.py:246
  61.1 6.2 %reshape.174 = f32[1024,512]{1,0:T(8,128)S(1)} reshape(f32[32,32,16,32]{3,2,1,0:T(8,128)} %copy.13) | data formatting | bytes 4194304 | tf_op jit(solution)/shard_map/reshape | solution.py:248
  67.3 1.0 slice_convert_fusion
  68.3 0.1 slice_add_fusion
  68.4 0.1 reshape.179
  68.5 0.1 fusion.3
  68.6 0.1 mul.47
  68.7 0.1 reshape.171
  68.8 1.6 %gather_fusion = f32[512,512]{1,0:T(8,128)S(1)} fusion(f32[1024,512]{1,0:T(8,128)S(1)} %reshape.174, s32[1024]{0:T(1024)S(1)} %pad_clamp_fusion), kind=kCustom, calls=%fused_computation | custom fusion | bytes 2099200 | tf_op jit(solution)/shard_map/jit(_take)/gather | solution.py:249
  70.5 0.1 fusion.2.target_ref
  70.6 21.9 %all-to-all-done = bf16[128,32,512]{2,1,0:T(8,128)(2,1)} async-done(((bf16[128,32,512]{2,1,0:T(8,128)(2,1)}), bf16[128,32,512]{2,1,0:T(8,128)(2,1)}, u32[]{:S(2)}, u32[]{:S(2)}) %all-to-all-start) | async-done | bytes 4194336 | tf_op jit(solution)/shard_map/all_to_all | solution.py:17
  92.5 4.4 %shard_map.66 = bf16[2048,128]{1,0:T(8,128)(2,1)S(1)} custom-call(bf16[4096,512]{1,0:T(8,128)(2,1)} %bitcast.x_hbm, s32[1,4096]{1,0:T(1,128)S(1)} %fusion.2.target_ref, f32[512,512]{1,0:T(8,128)S(1)} %gather_fusion), custom_call_target="tpu_custom_call" | custom-call | tf_op jit(solution)/shard_map/pallas_call | solution.py:163
  96.9 17.9 %all_to_all.15.x_ref = bf16[128,16,128]{2,1,0:T(8,128)(2,1)S(1)} all-to-all(bf16[128,16,128]{2,1,0:T(8,128)(2,1)S(1)} %bitcast.26), channel_id=1, replica_groups=mesh['group'=4,'chip'=16,'core'=2] {'group','chip','core'}, dimensions={0} | all-to-all | bytes 1048576 | tf_op jit(solution)/shard_map/all_to_all | solution.py:17
  114.8 1.3 %shard_map.67 = f32[4,256,256]{2,1,0:T(8,128)} custom-call(bf16[128,16,128]{2,1,0:T(8,128)(2,1)S(1)} %all_to_all.15.x_ref), custom_call_target="tpu_custom_call" | custom-call | tf_op jit(solution)/shard_map/pallas_call | solution.py:201
  (2 shorter events, 0.0 us)
Async XLA Ops:
  2.1 30.6 %all-to-all-start.1 = ((bf16[64,72,128]{2,1,0:T(8,128)(2,1)}), bf16[64,72,128]{2,1,0:T(8,128)(2,1)}, u32[]{:S(2)}, u32[]{:S(2)}) async-start(bf16[64,72,128]{2,1,0:T(8,128)(2,1)} %shard_map.65), calls=%async_computation.1 | async-start | bytes 2359296 | tf_op jit(solution)/shard_map/all_to_all | solution.py:17
  32.7 59.8 %all-to-all-start = ((bf16[128,32,512]{2,1,0:T(8,128)(2,1)}), bf16[128,32,512]{2,1,0:T(8,128)(2,1)}, u32[]{:S(2)}, u32[]{:S(2)}) async-start(bf16[128,32,512]{2,1,0:T(8,128)(2,1)} %shard_map.64), calls=%async_computation | async-start | bytes 8388608 | tf_op jit(solution)/shard_map/all_to_all | solution.py:17
  42.2 3.5 %collective-permute-start = (bf16[64,56,128]{2,1,0:T(8,128)(2,1)S(1)}, bf16[64,56,128]{2,1,0:T(8,128)(2,1)S(1)}, u32[]{:S(2)}, u32[]{:S(2)}) collective-permute-start(bf16[64,56,128]{2,1,0:T(8,128)(2,1)S(1)} %get-tuple-element.8), channel_id=1, source_target_pairs={{0,1},{1,0},{2,3},{3,2},{4,5},{5,4},{6,7},{7,6},{8,9},{9,8},{10,11... | collective-permute-start | bytes 2752520 | tf_op jit(solution)/shard_map/ppermute | solution.py:231
  46.2 1.3 %copy-start = (bf16[64,2,56,128]{3,2,1,0:T(8,128)(2,1)}, bf16[64,2,56,128]{3,2,1,0:T(8,128)(2,1)S(1)}, u32[]{:S(2)}) copy-start(bf16[64,2,56,128]{3,2,1,0:T(8,128)(2,1)S(1)} %copy.9) | copy-start | bytes 5505028

commit v4 on v3

--- a/solution.py
+++ b/solution.py
@@ -135,10 +135,12 @@
     )(a_tiles, scaling)
 
 
-def sum_kernel(x_hbm, target_ref, update_ref, out_ref, x_ref, spread_ref, sem_ref):
+def sum_kernel(x_hbm, target_ref, update_ref, *refs):
+    ready_refs, (out_ref, x_ref, spread_ref, sem_ref) = refs[:-4], refs[-4:]
     n_tiles, chunk = update_ref.shape
     parts = sem_ref.shape[0]
     share = x_ref.shape[0] // parts
+    own = parts - len(ready_refs)
     copies = []
     for n in range(parts):
         at = pl.ds(n * share, share)
@@ -148,7 +150,10 @@
     total = -update_ref[...]
     for n in range(parts):
         at = slice(n * share, (n + 1) * share)
-        picking = jnp.where(number == target_ref[:, at], 1.0, 0.0).astype(jnp.bfloat16)
+        if n < own:
+            picking = jnp.where(number == target_ref[:, at], 1.0, 0.0).astype(jnp.bfloat16)
+        else:
+            picking = ready_refs[n - own][...]
         copies[n].wait()
         total += jnp.dot(picking, x_ref[at, :], preferred_element_type=jnp.float32)
     pieces = chunk // LANES
@@ -159,19 +164,23 @@
 
 def sum_by_target(x, target, update):
     n_tiles, chunk = update.shape
+    parts, own = 4, 2
+    share = x.shape[0] // parts
+    number = jnp.arange(n_tiles, dtype=jnp.int32)[:, None]
+    ready = [(target[None, n * share:(n + 1) * share] == number).astype(jnp.bfloat16) for n in range(own, parts)]
     vmem = pl.BlockSpec(memory_space=pltpu.VMEM)
     return pl.pallas_call(
         sum_kernel,
-        in_specs=[pl.BlockSpec(memory_space=pltpu.HBM), vmem, vmem],
+        in_specs=[pl.BlockSpec(memory_space=pltpu.HBM)] + [vmem] * (2 + len(ready)),
         out_specs=vmem,
         out_shape=jax.ShapeDtypeStruct((n_tiles * chunk // LANES, LANES), jnp.bfloat16),
         scratch_shapes=[
             pltpu.VMEM(x.shape, x.dtype),
             pltpu.VMEM((n_tiles * chunk // LANES + 8, LANES), jnp.float32),
-            pltpu.SemaphoreType.DMA((4,)),
+            pltpu.SemaphoreType.DMA((parts,)),
         ],
-        compiler_params=VMEM,
-    )(x, target.reshape(1, -1), update)
+        compiler_params=pltpu.CompilerParams(vmem_limit_bytes=24 << 20),
+    )(x, target.reshape(1, -1), update, *ready)
 
 
 def final_kernel(n_down, n_across, x_ref, out_ref, spread_ref):

time: 117 us -> 117 us (level)
  no operation moved by 1% of the time
where the time goes in v4:
time: 117 us; the launch traced here: 116 us
  waiting for transfers between devices  30.6 us (26%)
  starting transfers between devices  20.6 us (18%)
  Pallas kernels  20.2 us (17%)
  local copies, waits for them, and re-layouts  18.8 us (16%)
  blocking collectives  17.9 us (15%)
  matrix products  4.63 us (4%)
  other arithmetic  2.94 us (3%)
    all_to_all x2, waiting for transfers between devices, exchange(): return lax.all_to_all(x, axes, split_axis=0, concat_axis=0, tiled=True)  28.5 us
    all_to_all x2, starting transfers between devices, exchange(): return lax.all_to_all(x, axes, split_axis=0, concat_axis=0, tiled=True)  19.2 us
    all_to_all x1, blocking collectives, exchange(): return lax.all_to_all(x, axes, split_axis=0, concat_axis=0, tiled=True)  17.9 us
    pallas_call x1, Pallas kernels, form_products(): pl.pallas_call(functools.partial(products_kernel, n_down, n_across), grid...  12.7 us
    transpose x1, local copies, waits for them, and re-layouts, per_device(): jnp.einsum('glrp,gsmp->lsrm', left, early[:, :, rows:rows + cols], prefer...  9.04 us
    reshape x1, local copies, waits for them, and re-layouts, per_device(): grid = jnp.einsum('glrp,gsmp->lsrm', left, early[:, :, rows:rows + cols],...  6.24 us
    dot_general x1, matrix products, per_device(): jnp.einsum('glrp,gsmp->lsrm', left, early[:, :, rows:rows + cols], prefer...  4.63 us
    pallas_call x1, Pallas kernels, sum_by_target(): pl.pallas_call(sum_kernel, in_specs=[pl.BlockSpec(memory_space=pltpu.HBM)...  4.14 us
  transfers between devices with their start and end apart: 3, of which 3 were waited for; matrix products, arithmetic and copies ran while one was open for 23% of the time, Pallas kernels for 11%

profile of v4, /device:TPU:1, one launch (start us, length us, event | category | flops | bytes accessed | tf_op | source)
XLA Modules:
  0.0 115.9 jit_solution(1375805603529363076)
XLA Ops:
  0.0 2.1 %shard_map.65 = bf16[64,72,128]{2,1,0:T(8,128)(2,1)} custom-call(s32[32]{0:T(128)} %bitcast.36, s32[32]{0:T(128)} %slot_hbm.1, s32[2,4]{1,0:T(2,128)} %bitcast.35, bf16[256,128]{1,0:T(8,128)(2,1)} %panel_hbm.1), custom_call_target="tpu_custom_call" | custom-call | tf_op jit(solution)/shard_map/pallas_call | solution.py:67
  2.1 12.2 %all-to-all-start.1 = ((bf16[64,72,128]{2,1,0:T(8,128)(2,1)}), bf16[64,72,128]{2,1,0:T(8,128)(2,1)}, u32[]{:S(2)}, u32[]{:S(2)}) async-start(bf16[64,72,128]{2,1,0:T(8,128)(2,1)} %shard_map.65), calls=%async_computation.1 | async-start | bytes 2359296 | tf_op jit(solution)/shard_map/all_to_all | solution.py:17
  14.3 12.7 %shard_map.64 = bf16[128,32,512]{2,1,0:T(8,128)(2,1)} custom-call(bf16[32,2,2,256,256]{4,3,2,1,0:T(8,128)(2,1)} %a_ref.1, f32[32,2,256]{2,1,0:T(2,128)} %scale_ref.1), custom_call_target="tpu_custom_call" | custom-call | tf_op jit(solution)/shard_map/pallas_call | solution.py:124
  27.0 5.7 %all-to-all-done.1 = bf16[64,72,128]{2,1,0:T(8,128)(2,1)} async-done(((bf16[64,72,128]{2,1,0:T(8,128)(2,1)}), bf16[64,72,128]{2,1,0:T(8,128)(2,1)}, u32[]{:S(2)}, u32[]{:S(2)}) %all-to-all-start.1) | async-done | bytes 1179680 | tf_op jit(solution)/shard_map/all_to_all | solution.py:17
  32.7 7.0 %all-to-all-start = ((bf16[128,32,512]{2,1,0:T(8,128)(2,1)}), bf16[128,32,512]{2,1,0:T(8,128)(2,1)}, u32[]{:S(2)}, u32[]{:S(2)}) async-start(bf16[128,32,512]{2,1,0:T(8,128)(2,1)} %shard_map.64), calls=%async_computation | async-start | bytes 8388608 | tf_op jit(solution)/shard_map/all_to_all | solution.py:17
  39.7 1.2 slice.52
  40.9 1.1 broadcast_select_fusion.1
  42.0 0.2 fusion.2
  42.2 1.4 %collective-permute-start = (bf16[64,56,128]{2,1,0:T(8,128)(2,1)S(1)}, bf16[64,56,128]{2,1,0:T(8,128)(2,1)S(1)}, u32[]{:S(2)}, u32[]{:S(2)}) collective-permute-start(bf16[64,56,128]{2,1,0:T(8,128)(2,1)S(1)} %get-tuple-element.8), channel_id=1, source_target_pairs={{0,1},{1,0},{2,3},{3,2},{4,5},{5,4},{6,7},{7,6},{8,9},{9,8},{10,11... | collective-permute-start | bytes 2752520 | tf_op jit(solution)/shard_map/ppermute | solution.py:240
  43.6 2.1 %collective-permute-done = bf16[64,56,128]{2,1,0:T(8,128)(2,1)S(1)} collective-permute-done((bf16[64,56,128]{2,1,0:T(8,128)(2,1)S(1)}, bf16[64,56,128]{2,1,0:T(8,128)(2,1)S(1)}, u32[]{:S(2)}, u32[]{:S(2)}) %collective-permute-start) | collective-permute-done | bytes 917536 | tf_op jit(solution)/shard_map/ppermute | solution.py:240
  45.7 0.3 maximum_select_fusion
  46.0 0.1 copy.9
  46.2 0.1 slice_convert_fusion
  46.2 0.1 fusion.12
  46.3 0.1 mul.60
  46.4 0.1 mul.54
  46.5 0.1 reshape.181
  46.6 0.1 reshape.177
  46.7 0.1 copy.11
  46.8 0.2 fusion.3
  47.0 4.6 %convolution_bitcast_fusion = f32[32,32,16,32]{0,3,2,1:T(8,128)} fusion(bf16[4,32,16,128,1]{3,1,0,2,4:T(8,128)(2,1)S(1)} %bitcast.34, bf16[4,32,56,128]{3,2,1,0:T(8,128)(2,1)S(1)} %bitcast.29), kind=kOutput, calls=%fused_computation.1 | convolution fusion | flops 536870912 | bytes 3670016 | tf_op jit(solution)/shard_map/glrp,gsmp->lsrm/dot_general | solution.py:255
  51.7 9.0 %copy.13 = f32[32,32,16,32]{3,2,1,0:T(8,128)} copy(f32[32,32,16,32]{0,3,2,1:T(8,128)} %convolution_bitcast_fusion) | data formatting | bytes 4194304 | tf_op jit(solution)/shard_map/glrp,gsmp->lsrm/transpose | solution.py:255
  60.7 6.2 %reshape.180 = f32[1024,512]{1,0:T(8,128)S(1)} reshape(f32[32,32,16,32]{3,2,1,0:T(8,128)} %copy.13) | data formatting | bytes 4194304 | tf_op jit(solution)/shard_map/reshape | solution.py:257
  67.0 0.1 slice_add_fusion
  67.1 0.1 reshape.186
  67.2 1.6 %gather_fusion = f32[512,512]{1,0:T(8,128)S(1)} fusion(f32[1024,512]{1,0:T(8,128)S(1)} %reshape.180, s32[1024]{0:T(1024)S(1)} %pad_clamp_fusion), kind=kCustom, calls=%fused_computation | custom fusion | bytes 2099200 | tf_op jit(solution)/shard_map/jit(_take)/gather | solution.py:258
  68.9 0.8 fusion
  69.6 0.1 fusion.4.target_ref
  69.8 22.7 %all-to-all-done = bf16[128,32,512]{2,1,0:T(8,128)(2,1)} async-done(((bf16[128,32,512]{2,1,0:T(8,128)(2,1)}), bf16[128,32,512]{2,1,0:T(8,128)(2,1)}, u32[]{:S(2)}, u32[]{:S(2)}) %all-to-all-start) | async-done | bytes 4194336 | tf_op jit(solution)/shard_map/all_to_all | solution.py:17
  92.5 4.1 %shard_map.66 = bf16[2048,128]{1,0:T(8,128)(2,1)S(1)} custom-call(bf16[4096,512]{1,0:T(8,128)(2,1)} %bitcast.x_hbm, s32[1,4096]{1,0:T(1,128)S(1)} %fusion.4.target_ref, f32[512,512]{1,0:T(8,128)S(1)} %gather_fusion, bf16[512,1024]{1,0:T(8,128)(2,1)S(1)} %get-tuple-element.13.refs_0_, bf16[512,1024]{1,0:T(8,128)(2,1)S(1)} %get-tuple-element.14.refs_1_), custom_call_target="tpu_custom_call" | custom-call | tf_op jit(solution)/shard_map/pallas_call | solution.py:172
  96.6 17.9 %all_to_all.15.x_ref = bf16[128,16,128]{2,1,0:T(8,128)(2,1)S(1)} all-to-all(bf16[128,16,128]{2,1,0:T(8,128)(2,1)S(1)} %bitcast.26), channel_id=1, replica_groups=mesh['group'=4,'chip'=16,'core'=2] {'group','chip','core'}, dimensions={0} | all-to-all | bytes 1048576 | tf_op jit(solution)/shard_map/all_to_all | solution.py:17
  114.5 1.3 %shard_map.67 = f32[4,256,256]{2,1,0:T(8,128)} custom-call(bf16[128,16,128]{2,1,0:T(8,128)(2,1)S(1)} %all_to_all.15.x_ref), custom_call_target="tpu_custom_call" | custom-call | tf_op jit(solution)/shard_map/pallas_call | solution.py:210
  (4 shorter events, 0.1 us)
Async XLA Ops:
  2.1 30.6 %all-to-all-start.1 = ((bf16[64,72,128]{2,1,0:T(8,128)(2,1)}), bf16[64,72,128]{2,1,0:T(8,128)(2,1)}, u32[]{:S(2)}, u32[]{:S(2)}) async-start(bf16[64,72,128]{2,1,0:T(8,128)(2,1)} %shard_map.65), calls=%async_computation.1 | async-start | bytes 2359296 | tf_op jit(solution)/shard_map/all_to_all | solution.py:17
  32.7 59.8 %all-to-all-start = ((bf16[128,32,512]{2,1,0:T(8,128)(2,1)}), bf16[128,32,512]{2,1,0:T(8,128)(2,1)}, u32[]{:S(2)}, u32[]{:S(2)}) async-start(bf16[128,32,512]{2,1,0:T(8,128)(2,1)} %shard_map.64), calls=%async_computation | async-start | bytes 8388608 | tf_op jit(solution)/shard_map/all_to_all | solution.py:17
  42.2 3.5 %collective-permute-start = (bf16[64,56,128]{2,1,0:T(8,128)(2,1)S(1)}, bf16[64,56,128]{2,1,0:T(8,128)(2,1)S(1)}, u32[]{:S(2)}, u32[]{:S(2)}) collective-permute-start(bf16[64,56,128]{2,1,0:T(8,128)(2,1)S(1)} %get-tuple-element.8), channel_id=1, source_target_pairs={{0,1},{1,0},{2,3},{3,2},{4,5},{5,4},{6,7},{7,6},{8,9},{9,8},{10,11... | collective-permute-start | bytes 2752520 | tf_op jit(solution)/shard_map/ppermute | solution.py:240
